TPU v7x, 32 devices: a whole 2x2x4 slice. The times are simulated.
32 devices in a mesh: head: 2 (over core), req: 16 (over z, y, x).
Axes of the slice: x: 2, y: 2, z: 4, core: 2. Of those that a mesh axis runs over, the one named last changes fastest.
Arguments:
- queries: bfloat16 [128, 8192], P('req', 'head'), may hold values from -9 to 9
- new_key: bfloat16 [128, 1024], P('req', 'head'), may hold values from -4 to 4
- new_value: bfloat16 [128, 1024], P('req', 'head'), may hold values from -4 to 4
- key_cache: bfloat16 [1472, 64, 1024], P('req', None, 'head'), may hold values from -4 to 4
- value_cache: bfloat16 [1472, 64, 1024], P('req', None, 'head'), may hold values from -4 to 4
- lengths: int32 [128], P('req'), may hold values from 1 to 4096, as said below
- page_table: int32 [128, 64], P('req'), may hold values from 0 to 91, as said below
- residual: bfloat16 [128, 8192], P(None, ('head', 'req')), may hold values from -6 to 6
- out_weight: bfloat16 [8192, 8192], P(None, ('head', 'req')), may hold values from -0.25 to 0.25
- gate_weight: bfloat16 [8192, 28672], P('head', 'req'), may hold values from -0.0625 to 0.0625
- up_weight: bfloat16 [8192, 28672], P('head', 'req'), may hold values from -0.0625 to 0.0625
- down_weight: bfloat16 [28672, 8192], P('req', 'head'), may hold values from -0.046875 to 0.046875
Outputs:
- layer_out: bfloat16 [128, 8192], P(None, ('head', 'req'))
Inputs may be any that keep to these rules, and one draw needn't show every extreme that they name: `lengths`: the 8 requests of one index of req hold at most one request of length 4096 and all others at most 256; each such group holds one request of length exactly 256, and some group holds one of length 4096. `page_table`: for request r the first ceil(lengths[r] / 64) entries name distinct pages of the pool of index r // 8 of req, and no page serves two requests; the other entries are arbitrary offsets and are not read.
All inputs are finite; a program needn't handle non-finite values.
Results may differ from a plain program's by a relative error of at most 0.01.
Values may be sent and summed in bfloat16 or wider, within the bound.
A program may use at most 192 MiB of HBM per device.

v0:
```python
import jax
import jax.numpy as jnp
from jax import lax
from jax.sharding import PartitionSpec as P

HD = 128


def attend_padded(queries, new_key, new_value, key_pool, value_pool, lengths, page_table):
    row_count = queries.shape[0]
    kv_width = key_pool.shape[2]
    groups = kv_width // HD
    per_group = queries.shape[1] // kv_width
    key_span = page_table.shape[1] * key_pool.shape[1]
    key_rows = key_pool[page_table].reshape(row_count, key_span, groups, HD)
    value_rows = value_pool[page_table].reshape(row_count, key_span, groups, HD)
    grouped = queries.reshape(row_count, groups, per_group, HD)
    scores = jnp.einsum(
        "rgqd,rtgd->rgqt", grouped, key_rows, preferred_element_type=jnp.float32
    ) * HD ** (-0.5)
    own_score = jnp.einsum(
        "rgqd,rgd->rgq",
        grouped,
        new_key.reshape(row_count, groups, HD),
        preferred_element_type=jnp.float32,
    ) * HD ** (-0.5)
    live_mask = (lax.broadcasted_iota(jnp.int32, (row_count, key_span), 1) < lengths[:, None])[
        :, None, None, :
    ]
    top_score = jnp.maximum(jnp.max(jnp.where(live_mask, scores, -1e30), axis=3), own_score)
    exp_terms = jnp.where(live_mask, jnp.exp(scores - top_score[..., None]), 0.0)
    own_exp = jnp.exp(own_score - top_score)
    total_mass = jnp.sum(exp_terms, axis=3) + own_exp
    weights = (exp_terms / total_mass[..., None]).astype(jnp.bfloat16)
    own_weight = (own_exp / total_mass).astype(jnp.bfloat16)
    summed = jnp.einsum("rgqt,rtgd->rgqd", weights, value_rows, preferred_element_type=jnp.float32)
    summed = summed + own_weight.astype(jnp.float32)[..., None] * new_value.reshape(
        row_count, groups, 1, HD
    ).astype(jnp.float32)
    return summed.reshape(row_count, -1).astype(jnp.bfloat16)


def body(
    queries,
    new_key,
    new_value,
    key_cache,
    value_cache,
    lengths,
    page_table,
    residual,
    out_weight,
    gate_weight,
    up_weight,
    down_weight,
):
    attention = attend_padded(
        queries, new_key, new_value, key_cache, value_cache, lengths, page_table
    )
    features = lax.all_gather(attention, "head", axis=1, tiled=True)
    attn_update = jnp.dot(
        lax.all_gather(features, "req", axis=0, tiled=True),
        out_weight,
        preferred_element_type=jnp.float32,
    )
    mixed_rows = (residual.astype(jnp.float32) + attn_update).astype(jnp.bfloat16)
    shard_piece = lax.all_gather(mixed_rows, "req", axis=1, tiled=True)
    gate_acts = jnp.dot(shard_piece, gate_weight, preferred_element_type=jnp.float32)
    up_acts = jnp.dot(shard_piece, up_weight, preferred_element_type=jnp.float32)
    gate_full, up_full = lax.psum((gate_acts, up_acts), "head")
    hidden = (jax.nn.silu(gate_full) * up_full).astype(jnp.bfloat16)
    down_part = lax.psum_scatter(
        lax.dot_general(
            down_weight, hidden, (((0,), (1,)), ((), ())), preferred_element_type=jnp.float32
        ),
        "req",
        scatter_dimension=0,
        tiled=True,
    )
    return (mixed_rows.astype(jnp.float32) + down_part.T).astype(jnp.bfloat16)


def solution(mesh):
    return jax.shard_map(
        body,
        mesh=mesh,
        in_specs=(
            P("req", "head"),
            P("req", "head"),
            P("req", "head"),
            P("req", None, "head"),
            P("req", None, "head"),
            P("req"),
            P("req", None),
            P(None, ("head", "req")),
            P(None, ("head", "req")),
            P("head", "req"),
            P("head", "req"),
            P("req", "head"),
        ),
        out_specs=P(None, ("head", "req")),
        check_vma=False,
    )
```

profile of v0, /device:TPU:0, one launch (start us, length us, event | category | flops | bytes accessed | tf_op | source)
XLA Modules:
  0.0 439.7 jit_solution(7683109631551850060)
XLA Ops:
  6.5 0.8 iota_compare_fusion
  7.3 0.7 compare_select_fusion
  8.0 0.1 reshape.49
  8.1 18.9 %gather_fusion = bf16[512,64,512]{2,1,0:T(8,128)(2,1)} fusion(bf16[92,64,512]{2,1,0:T(8,128)(2,1)} %param.15, s32[1024]{0:T(1024)S(1)} %pad_clamp_fusion), kind=kCustom, calls=%fused_computation | custom fusion | bytes 67110912 | tf_op jit(solution)/shard_map/gather | solution.py:15
  26.9 46.0 %reshape.42 = bf16[8,4096,4,128]{3,2,1,0:T(4,128)(2,1)} reshape(bf16[512,64,512]{2,1,0:T(8,128)(2,1)} %gather_fusion) | data formatting | bytes 67108864 | tf_op jit(solution)/shard_map/reshape | solution.py:15
  73.0 0.2 fusion.31
  73.1 18.8 %select_reduce_fusion = (f32[8,4,8]{2,1,0:T(4,128)S(1)}, f32[8,4,4096,8]{2,3,1,0:T(8,128)S(1)}) fusion(pred[8,4096]{1,0:T(8,128)(4,1)S(1)} %iota_compare_fusion, bf16[8,4,8,128]{3,0,2,1:T(8,128)(2,1)S(1)} %bitcast.45, bf16[8,4096,4,128]{3,2,1,0:T(4,128)(2,1)} %reshape.42), kind=kOutput, calls=%fused_computation.12 | convolution fusion | flops 271580928 | bytes 37848064 | tf_op jit(solution)/shard_map/rgqd,rtgd->rgqt/dot_general | solution.py:18
  92.0 2.0 copy-done.3
  94.0 1.0 bitcast_reduce_fusion
  95.0 19.0 %gather_fusion.1 = bf16[512,64,512]{2,1,0:T(8,128)(2,1)} fusion(bf16[92,64,512]{2,1,0:T(8,128)(2,1)} %param.16, s32[1024]{0:T(1024)S(1)} %pad_clamp_fusion), kind=kCustom, calls=%fused_computation.1 | custom fusion | bytes 67110912 | tf_op jit(solution)/shard_map/gather | solution.py:16
  114.0 46.0 %reshape.45 = bf16[8,4096,4,128]{3,2,1,0:T(4,128)(2,1)} reshape(bf16[512,64,512]{2,1,0:T(8,128)(2,1)} %gather_fusion.1) | data formatting | bytes 67108864 | tf_op jit(solution)/shard_map/reshape | solution.py:16
  160.1 20.0 %fusion.24 = bf16[1,8,32,128]{3,2,1,0:T(8,128)(2,1)S(1)} fusion(bf16[8,4096,4,128]{3,2,1,0:T(4,128)(2,1)} %reshape.45, f32[8,4,4096,8]{2,3,1,0:T(8,128)} %copy-done.3, f32[8,4,8]{2,1,0:T(4,128)S(1)} %get-tuple-element.8, f32[8,4,8]{2,1,0:T(4,128)S(1)} %multiply_maximum_fusion, pred[8,4096]{1,0:T(8,128)(4,1)S(1)} %iota_compare_fusion, ...), kind=kOutput, calls=%fused_computation.21 | convolution fusion | flops 272728064 | bytes 37866496 | tf_op jit(solution)/shard_map/rgqt,rtgd->rgqd/dot_general | solution.py:36
  180.1 2.1 all_gather.9
  182.3 0.0 all-gather.5.cloned.1.call-start
  182.3 63.4 %all-gather.3.cloned.1.call-done = bf16[128,8192]{1,0:T(8,128)(2,1)} async-done(((bf16[8,8192]{1,0:T(8,128)(2,1)}), bf16[128,8192]{1,0:T(8,128)(2,1)}) %all-gather.3.cloned.1.call-update) | async-done | bytes 2097168 | tf_op jit(solution)/shard_map/all_gather | solution.py:62
  245.7 4.2 fusion.23
  249.9 0.0 all-reduce.3.cloned.1.call-start
  249.9 53.8 %all-gather.5.cloned.1.call-done = bf16[128,4096]{1,0:T(8,128)(2,1)} async-done(((bf16[128,256]{1,0:T(8,128)(2,1)}), bf16[128,4096]{1,0:T(8,128)(2,1)}) %all-gather.5.cloned.1.call-update) | async-done | bytes 1048592 | tf_op jit(solution)/shard_map/all_gather | solution.py:67
  303.8 8.6 %fusion.39 = f32[128,1792]{1,0:T(8,128)} fusion(bf16[128,4096]{1,0:T(8,128)(2,1)} %all-gather.5.cloned.1.call-done, bf16[4096,1792]{1,0:T(8,128)(2,1)} %param.21), kind=kOutput, calls=%fused_computation.42 | convolution fusion | flops 1879048192 | bytes 16646144 | tf_op jit(solution)/shard_map/dot_general | solution.py:68
  312.4 8.2 %fusion.40 = f32[128,1792]{1,0:T(8,128)} fusion(bf16[128,4096]{1,0:T(8,128)(2,1)S(1)} %copy-done.2, bf16[4096,1792]{1,0:T(8,128)(2,1)} %param.22), kind=kOutput, calls=%fused_computation.43 | convolution fusion | flops 1879048192 | bytes 16646144 | tf_op jit(solution)/shard_map/dot_general | solution.py:69
  320.7 19.8 %all-reduce.3.cloned.1.call-done = (f32[128,1792]{1,0:T(8,128)}, f32[128,1792]{1,0:T(8,128)}) async-done(((f32[128,1792]{1,0:T(8,128)}, f32[128,1792]{1,0:T(8,128)}), (f32[128,1792]{1,0:T(8,128)}, f32[128,1792]{1,0:T(8,128)})) %all-reduce.3.cloned.1.call-update) | async-done | bytes 1835024 | tf_op jit(solution)/shard_map/psum | solution.py:70
  340.5 9.2 %convolution_bitcast_fusion = f32[4096,128]{0,1:T(8,128)} fusion(bf16[1792,4096]{1,0:T(8,128)(2,1)} %param.23, f32[128,1792]{1,0:T(8,128)} %get-tuple-element.5, f32[128,1792]{1,0:T(8,128)} %get-tuple-element.6), kind=kOutput, calls=%fused_computation.7 | convolution fusion | flops 1880424448 | bytes 18612224 | tf_op jit(solution)/shard_map/dot_general | solution.py:73
  349.8 81.9 %reduce-scatter.2.cloned.1.call-done = f32[256,128]{0,1:T(8,128)} async-done(((f32[4096,128]{0,1:T(8,128)}), f32[256,128]{0,1:T(8,128)}) %reduce-scatter.2.cloned.1.call-update) | async-done | bytes 131088 | tf_op jit(solution)/shard_map/reduce_scatter | solution.py:72
  431.7 1.6 fusion.30
  (27 shorter events, 0.2 us)
Async XLA Ops:
  6.5 66.4 %copy-start = (bf16[8,512]{1,0:T(8,128)(2,1)S(1)}, bf16[8,512]{1,0:T(8,128)(2,1)}, u32[]{:S(2)}) copy-start(bf16[8,512]{1,0:T(8,128)(2,1)} %param.13) | copy-start | bytes 24580
  6.5 239.2 %all-gather.3.cloned.1.call-start = ((), (), s32[]{:S(2)}) async-start(), calls=%async_computation.1 | async-start | bytes 2228224 | tf_op jit(solution)/shard_map/all_gather | solution.py:62
  26.9 46.0 %copy-start.7 = (bf16[8,4096]{1,0:T(8,128)(2,1)S(1)}, bf16[8,4096]{1,0:T(8,128)(2,1)}, u32[]{:S(2)}) copy-start(bf16[8,4096]{1,0:T(8,128)(2,1)} %param.12) | copy-start | bytes 196612
  92.0 2.0 copy-start.3
  114.0 46.0 %copy-start.6 = (bf16[8,512]{1,0:T(8,128)(2,1)S(1)}, bf16[8,512]{1,0:T(8,128)(2,1)}, u32[]{:S(2)}) copy-start(bf16[8,512]{1,0:T(8,128)(2,1)} %param.14) | copy-start | bytes 24580
  160.1 85.6 %copy-start.5 = (bf16[128,256]{1,0:T(8,128)(2,1)S(1)}, bf16[128,256]{1,0:T(8,128)(2,1)}, u32[]{:S(2)}) copy-start(bf16[128,256]{1,0:T(8,128)(2,1)} %param.19) | copy-start | bytes 196612
  182.3 121.5 %all-gather.5.cloned.1.call-start = ((), (), s32[]{:S(2)}) async-start(), calls=%async_computation.2 | async-start | bytes 1114112 | tf_op jit(solution)/shard_map/all_gather | solution.py:67
  249.9 90.6 %all-reduce.3.cloned.1.call-start = ((), (), s32[]{:S(2)}) async-start(), calls=%async_computation.4 | async-start | bytes 3670016 | tf_op jit(solution)/shard_map/psum | solution.py:70
  303.8 8.6 %copy-start.2 = (bf16[128,4096]{1,0:T(8,128)(2,1)S(1)}, bf16[128,4096]{1,0:T(8,128)(2,1)}, u32[]{:S(2)}) copy-start(bf16[128,4096]{1,0:T(8,128)(2,1)} %all-gather.5.cloned.1.call-done) | copy-start | bytes 3145732
  320.6 111.0 %reduce-scatter.2.cloned.1.call-start = ((), (), s32[]{:S(2)}) async-start(), calls=%async_computation.3 | async-start | bytes 2228224 | tf_op jit(solution)/shard_map/reduce_scatter | solution.py:72
  340.5 91.1 %copy-start.4 = (bf16[128,256]{1,0:T(8,128)(2,1)S(1)}, bf16[128,256]{1,0:T(8,128)(2,1)}, u32[]{:S(2)}) copy-start(bf16[128,256]{1,0:T(8,128)(2,1)} %fusion.23) | copy-start | bytes 196612
  340.5 92.7 %copy-start.1 = (bf16[8,512]{1,0:T(8,128)(2,1)S(1)}, bf16[8,512]{1,0:T(8,128)(2,1)}, u32[]{:S(2)}) copy-start(bf16[8,512]{1,0:T(8,128)(2,1)} %param.13) | copy-start | bytes 24580
Sparse Core Ops, SparseCore 0:
  182.4 63.2 all-gather.2
  250.0 53.7 all-gather.4
  320.7 19.7 all-reduce.2
  349.9 81.7 reduce-scatter.1
where the time goes:
time: 442 us; the launch traced here: 440 us
  waiting for transfers between devices  219 us (50%)
  local copies, waits for them, and re-layouts  132 us (30%)
  matrix products  69.2 us (16%)
  between operations  13.2 us (3%)
    reduce_scatter x1, waiting for transfers between devices, body(): lax.psum_scatter(lax.dot_general(down_weight, hidden, (((0,), (1,)), ((),...  81.9 us
    all_gather x1, waiting for transfers between devices, body(): lax.all_gather(features, 'req', axis=0, tiled=True)  63.4 us
    all_gather x1, waiting for transfers between devices, body(): shard_piece = lax.all_gather(mixed_rows, 'req', axis=1, tiled=True)  53.8 us
    reshape x1, local copies, waits for them, and re-layouts, attend_padded(): key_rows = key_pool[page_table].reshape(row_count, key_span, groups, HD)  46 us
    reshape x1, local copies, waits for them, and re-layouts, attend_padded(): value_rows = value_pool[page_table].reshape(row_count, key_span, groups, HD)  46 us
    dot_general x1, matrix products, attend_padded(): jnp.einsum('rgqt,rtgd->rgqd', weights, value_rows, preferred_element_type...  20 us
    psum x1, waiting for transfers between devices, body(): gate_full, up_full = lax.psum((gate_acts, up_acts), 'head')  19.8 us
    gather x1, local copies, waits for them, and re-layouts, attend_padded(): value_rows = value_pool[page_table].reshape(row_count, key_span, groups, HD)  19 us
  transfers between devices with their start and end apart: 4, of which 4 were waited for; matrix products, arithmetic and copies ran while one was open for 0% of the time, Pallas kernels for 0%

commit v1 on v0

v1 whole, which is shorter than its diff:
```python
import functools

import jax
import jax.numpy as jnp
from jax import lax
from jax.experimental import pallas as pl
from jax.experimental.pallas import tpu as pltpu
from jax.sharding import PartitionSpec as P

HD = 128
MESH = pl.DeviceIdType.MESH
F32, BF16 = jnp.float32, jnp.bfloat16
NT = (((1,), (1,)), ((), ()))


def attend_kernel(
    short_pages, lengths, table, q_ref, nk_ref, nv_ref, keys, values, out_ref,
    ks, vs, kl, vl, s_ref, sl_ref, o_ref, sems,
):
    reqs, slots = table.shape
    page = keys.shape[1]
    groups = nk_ref.shape[0] // reqs
    per = q_ref.shape[0] // nk_ref.shape[0]
    span = short_pages * page
    block = groups * per
    scale = HD ** -0.5

    def start_short(r, carry):
        for i in range(short_pages):
            p = table[r, i]
            pltpu.make_async_copy(keys.at[p], ks.at[r, i], sems.at[0]).start()
            pltpu.make_async_copy(values.at[p], vs.at[r, i], sems.at[1]).start()
        return carry

    lax.fori_loop(0, reqs, start_short, 0)
    long_r = jnp.int32(-1)
    for r in range(reqs):
        long_r = jnp.where(lengths[r] > span, jnp.int32(r), long_r)
    has_long = long_r >= 0
    row = jnp.maximum(long_r, 0)

    @pl.when(has_long)
    def _():
        def start_long(i, carry):
            p = table[row, i]
            pltpu.make_async_copy(keys.at[p], kl.at[i], sems.at[2]).start()
            pltpu.make_async_copy(values.at[p], vl.at[i], sems.at[3]).start()
            return carry

        lax.fori_loop(0, slots, start_long, 0)

    def spread(ref):
        v = ref[...]
        return jnp.broadcast_to(v[:, None, :], (reqs * groups, per, HD)).reshape(-1, HD)

    q = q_ref[...]
    own = jnp.sum(q * spread(nk_ref), axis=1, keepdims=True) * scale
    new_v = spread(nv_ref)
    o_ref[...] = own * jnp.ones((1, HD), F32)

    pltpu.make_async_copy(ks, ks, sems.at[0]).wait()
    for r in range(reqs):
        for g in range(groups):
            at = r * block + g * per
            k = ks[r, :, :, g * HD:(g + 1) * HD].reshape(span, HD)
            s_ref[at:at + per, :] = lax.dot_general(
                q_ref[at:at + per, :].astype(BF16), k, NT, preferred_element_type=F32
            ) * scale
    pltpu.make_async_copy(vs, vs, sems.at[1]).wait()
    pos = lax.broadcasted_iota(jnp.int32, (block, span), 1)
    for r in range(reqs):
        rows = slice(r * block, (r + 1) * block)
        live = pos < lengths[r]
        s = jnp.where(live, s_ref[rows, :], -1e30)
        mine = own[rows]
        top = jnp.maximum(jnp.max(s, axis=1, keepdims=True), mine)
        e = jnp.where(live, jnp.exp(s - top), 0.0)
        own_e = jnp.exp(mine - top)
        inv = 1.0 / (jnp.sum(e, axis=1, keepdims=True) + own_e)
        s_ref[rows, :] = e * inv
        o_ref[rows, :] = (own_e * inv).astype(BF16).astype(F32) * new_v[rows]
    for r in range(reqs):
        for g in range(groups):
            at = r * block + g * per
            v = vs[r, :, :, g * HD:(g + 1) * HD].reshape(span, HD)
            o_ref[at:at + per, :] += jnp.dot(
                s_ref[at:at + per, :].astype(BF16), v, preferred_element_type=F32
            )

    @pl.when(has_long)
    def _():
        full = slots * page
        base = pl.multiple_of(row * block, block)
        pltpu.make_async_copy(kl, kl, sems.at[2]).wait()
        ql = q_ref[pl.ds(base, block), :]
        for g in range(groups):
            k = kl[:, :, g * HD:(g + 1) * HD].reshape(full, HD)
            sl_ref[g * per:(g + 1) * per, :] = lax.dot_general(
                ql[g * per:(g + 1) * per].astype(BF16), k, NT, preferred_element_type=F32
            ) * scale
        nkl = nk_ref[pl.ds(row * groups, groups), :]
        nvl = nv_ref[pl.ds(row * groups, groups), :]
        nkl = jnp.broadcast_to(nkl[:, None, :], (groups, per, HD)).reshape(block, HD)
        nvl = jnp.broadcast_to(nvl[:, None, :], (groups, per, HD)).reshape(block, HD)
        mine = jnp.sum(ql * nkl, axis=1, keepdims=True) * scale
        live = lax.broadcasted_iota(jnp.int32, (block, full), 1) < lengths[row]
        s = jnp.where(live, sl_ref[...], -1e30)
        top = jnp.maximum(jnp.max(s, axis=1, keepdims=True), mine)
        e = jnp.where(live, jnp.exp(s - top), 0.0)
        own_e = jnp.exp(mine - top)
        inv = 1.0 / (jnp.sum(e, axis=1, keepdims=True) + own_e)
        sl_ref[...] = e * inv
        added = (own_e * inv).astype(BF16).astype(F32) * nvl
        pltpu.make_async_copy(vl, vl, sems.at[3]).wait()
        parts = []
        for g in range(groups):
            v = vl[:, :, g * HD:(g + 1) * HD].reshape(full, HD)
            parts.append(jnp.dot(
                sl_ref[g * per:(g + 1) * per, :].astype(BF16), v, preferred_element_type=F32
            ))
        o_ref[pl.ds(base, block), :] = jnp.concatenate(parts, axis=0) + added

    out_ref[...] = o_ref[...].astype(BF16)


def attend(queries, new_key, new_value, keys, values, lengths, table):
    reqs, slots = table.shape
    _, page, width = keys.shape
    groups = width // HD
    short = min(4, slots)
    rows = queries.shape[1] // HD * reqs
    per_req = rows // reqs
    smem = pl.BlockSpec(memory_space=pltpu.SMEM)
    vmem = pl.BlockSpec(memory_space=pltpu.VMEM)
    hbm = pl.BlockSpec(memory_space=pl.ANY)
    out = pl.pallas_call(
        functools.partial(attend_kernel, short),
        out_shape=jax.ShapeDtypeStruct((rows, HD), BF16),
        in_specs=[smem, smem, vmem, vmem, vmem, hbm, hbm],
        out_specs=vmem,
        scratch_shapes=[
            pltpu.VMEM((reqs, short, page, width), BF16),
            pltpu.VMEM((reqs, short, page, width), BF16),
            pltpu.VMEM((slots, page, width), BF16),
            pltpu.VMEM((slots, page, width), BF16),
            pltpu.VMEM((rows, short * page), F32),
            pltpu.VMEM((per_req, slots * page), F32),
            pltpu.VMEM((rows, HD), F32),
            pltpu.SemaphoreType.DMA((4,)),
        ],
        compiler_params=pltpu.CompilerParams(vmem_limit_bytes=40 * 2**20),
        name="attend",
    )(
        lengths, table,
        queries.astype(F32).reshape(rows, HD),
        new_key.astype(F32).reshape(reqs * groups, HD),
        new_value.astype(F32).reshape(reqs * groups, HD),
        keys, values,
    )
    half = per_req // 2
    return out.reshape(reqs, 2, half, HD).transpose(1, 0, 2, 3).reshape(2 * reqs, half * HD)


def layer_kernel(
    A, B, att_ref, res_ref, wo_hbm, wg_hbm, wu_hbm, wd_hbm, out_ref,
    wo, wg, wu, wd, att, mix, acc_g, acc_u, xs, xr, hid, pf, ps, r1, zs, r2,
    wsem, sa, ra, sb, rb, ss, rs, sma, rma, smb, rmb, sx, rx, s1, g1, s2, g2,
):
    h = lax.axis_index("head")
    idx = lax.axis_index("req")
    a, b = idx // B, lax.rem(idx, B)
    n = A * B
    rows, c = res_ref.shape
    reqs = att_ref.shape[0] // 2
    kh = att_ref.shape[1]
    tiles, _, tile = acc_g.shape

    def far(da):
        return {"req": lax.rem(a + da, A) * B + b}

    def near(db):
        return {"req": a * B + lax.rem(b + db, B)}

    sibling = {"head": 1 - h}

    loads = [
        pltpu.make_async_copy(x, y, wsem.at[i])
        for i, (x, y) in enumerate(((wo_hbm, wo), (wg_hbm, wg), (wu_hbm, wu), (wd_hbm, wd)))
    ]
    for l in loads:
        l.start()

    barrier = pltpu.get_barrier_semaphore()
    for peer in [far(i) for i in range(1, A)] + [near(i) for i in range(1, B)] + [sibling]:
        pl.semaphore_signal(barrier, inc=1, device_id=peer, device_id_type=MESH)
    att[0, idx] = att_ref[...]
    pl.semaphore_wait(barrier, A + B - 1)

    def send(src, dst, s, r, to):
        cp = pltpu.make_async_remote_copy(
            src_ref=src, dst_ref=dst, send_sem=s, recv_sem=r, device_id=to, device_id_type=MESH
        )
        cp.start()
        return cp

    def source(da, db):
        return lax.rem(a + A - da, A) * B + lax.rem(b + B - db, B)

    def gather_start(ref, sfar, rfar, snear, rnear, each):
        fars = [None] + [
            send(ref.at[idx], ref.at[idx], sfar.at[d], rfar.at[d], far(d)) for d in range(1, A)
        ]
        nears = {}
        for da in range(A):
            if da:
                fars[da].wait_recv()
            at = source(da, 0)
            for db in range(1, B):
                nears[da, db] = send(
                    ref.at[at], ref.at[at], snear.at[da, db], rnear.at[da, db], near(db)
                )
            each(da, at)
        return fars, nears

    forwards = {}

    def forward(da, db, at):
        forwards[da, db] = send(
            att.at[0, at], att.at[1, at], ss.at[da, db], rs.at[da, db], sibling
        )

    fars, nears = gather_start(
        att.at[0], sa, ra, sb, rb, lambda da, at: forward(da, 0, at)
    )
    for da in range(A):
        for db in range(1, B):
            nears[da, db].wait_recv()
            forward(da, db, source(da, db))

    loads[0].wait()

    def project(slot, side):
        total = None
        lhs = att[slot].reshape(n * 2 * reqs, kh)
        for j in range(2):
            w = wo[pl.ds(pl.multiple_of((side * 2 + j) * kh, kh), kh), :]
            r = jnp.dot(lhs, w, preferred_element_type=F32)
            r = r.reshape(n, 2 * reqs, c)[:, j * reqs:(j + 1) * reqs].reshape(n * reqs, c)
            total = r if total is None else total + r
        return total

    update = project(0, h)
    for cp in forwards.values():
        cp.wait_recv()
    update = update + project(1, 1 - h)
    mix[idx] = (res_ref[...].astype(F32) + update).astype(BF16)

    mfars = [None] + [
        send(mix.at[idx], mix.at[idx], sma.at[d], rma.at[d], far(d)) for d in range(1, A)
    ]
    mnears = {}

    def spread(da):
        if da:
            mfars[da].wait_recv()
        at = source(da, 0)
        for db in range(1, B):
            mnears[da, db] = send(
                mix.at[at], mix.at[at], smb.at[da, db], rmb.at[da, db], near(db)
            )

    spread(0)
    loads[1].wait()
    loads[2].wait()
    for da in range(A):
        for db in range(1, B):
            mnears[da, db].wait_recv()
        if da + 1 < A:
            spread(da + 1)
        group = lax.rem(a + A - da, A) * B

        def do_tile(t, carry, da=da, group=group):
            cols = pl.ds(pl.multiple_of(t * tile, tile), tile) if tiles > 1 else slice(None)
            g = u = None
            for k in range(B):
                lhs = mix[group + k]
                at = pl.ds(pl.multiple_of((group + k) * c, c), c)
                gk = jnp.dot(lhs, wg[at, cols], preferred_element_type=F32)
                uk = jnp.dot(lhs, wu[at, cols], preferred_element_type=F32)
                g = gk if g is None else g + gk
                u = uk if u is None else u + uk
            if da:
                g = g + acc_g[t]
                u = u + acc_u[t]
            acc_g[t] = g
            acc_u[t] = u
            if da == A - 1:
                xs[t, 0] = g.astype(BF16)
                xs[t, 1] = u.astype(BF16)
                send(xs.at[t], xr.at[t], sx.at[t], rx.at[t], sibling)
            return carry

        lax.fori_loop(0, tiles, do_tile, 0)

    for t in range(tiles):
        pltpu.make_async_remote_copy(
            src_ref=xs.at[t], dst_ref=xr.at[t], send_sem=sx.at[t], recv_sem=rx.at[t],
            device_id=sibling, device_id_type=MESH,
        ).wait()
        g = acc_g[t] + xr[t, 0].astype(F32)
        u = acc_u[t] + xr[t, 1].astype(F32)
        hid[:, t * tile:(t + 1) * tile] = (g / (1.0 + jnp.exp(-g)) * u).astype(BF16)

    loads[3].wait()
    width = max(c, min(256, B * c))
    inner = width // c
    firsts, seconds = {}, []

    def reduce(i):
        total = pf[i % 2, b]
        for db in range(1, B):
            firsts[i, db].wait_recv()
            total = total + r1[i, db].astype(F32)
        return total

    def pass_on(i):
        zs[i] = reduce(i).astype(BF16)
        seconds.append(send(zs.at[i], r2.at[i], s2.at[i], g2.at[i], far(i + 1)))

    for i in range(A):
        ta = lax.rem(a + 1 + i, A)

        def do_cols(k, carry, i=i, ta=ta):
            cols = pl.ds(pl.multiple_of(ta * (B * c) + k * width, width), width)
            r = jnp.dot(hid[...], wd[:, cols], preferred_element_type=F32)
            for m in range(inner):
                piece = r[:, m * c:(m + 1) * c]
                pf[i % 2, k * inner + m] = piece
                ps[i, k * inner + m] = piece.astype(BF16)
            return carry

        lax.fori_loop(0, B // inner, do_cols, 0)
        for db in range(1, B):
            firsts[i, db] = send(
                ps.at[i, lax.rem(b + db, B)], r1.at[i, db], s1.at[i, db], g1.at[i, db], near(db)
            )
        if i:
            pass_on(i - 1)
    total = mix[idx].astype(F32) + reduce(A - 1)
    for i, cp in enumerate(seconds):
        cp.wait_recv()
        total = total + r2[i].astype(F32)
    out_ref[...] = total.astype(BF16)

    for cp in (
        fars[1:] + list(nears.values()) + list(forwards.values()) + mfars[1:]
        + list(mnears.values()) + list(firsts.values()) + seconds
    ):
        cp.wait_send()


def layer(n, att, residual, wo, wg, wu, wd):
    A = 4 if n % 4 == 0 else 1
    B = n // A
    rows, c = residual.shape
    ff = wg.shape[1]
    tile = 256 if ff % 256 == 0 else ff
    tiles = ff // tile
    vmem = pl.BlockSpec(memory_space=pltpu.VMEM)
    hbm = pl.BlockSpec(memory_space=pl.ANY)
    dma = pltpu.SemaphoreType.DMA
    return pl.pallas_call(
        functools.partial(layer_kernel, A, B),
        out_shape=jax.ShapeDtypeStruct((rows, c), BF16),
        in_specs=[vmem, vmem, hbm, hbm, hbm, hbm],
        out_specs=vmem,
        scratch_shapes=[
            pltpu.VMEM(wo.shape, BF16),
            pltpu.VMEM(wg.shape, BF16),
            pltpu.VMEM(wu.shape, BF16),
            pltpu.VMEM(wd.shape, BF16),
            pltpu.VMEM((2, n) + att.shape, BF16),
            pltpu.VMEM((n, rows, c), BF16),
            pltpu.VMEM((tiles, rows, tile), F32),
            pltpu.VMEM((tiles, rows, tile), F32),
            pltpu.VMEM((tiles, 2, rows, tile), BF16),
            pltpu.VMEM((tiles, 2, rows, tile), BF16),
            pltpu.VMEM((rows, ff), BF16),
            pltpu.VMEM((2, B, rows, c), F32),
            pltpu.VMEM((A, B, rows, c), BF16),
            pltpu.VMEM((A, B, rows, c), BF16),
            pltpu.VMEM((A, rows, c), BF16),
            pltpu.VMEM((A, rows, c), BF16),
            dma((4,)),
            dma((A,)), dma((A,)), dma((A, B)), dma((A, B)), dma((A, B)), dma((A, B)),
            dma((A,)), dma((A,)), dma((A, B)), dma((A, B)),
            dma((tiles,)), dma((tiles,)),
            dma((A, B)), dma((A, B)), dma((A,)), dma((A,)),
        ],
        compiler_params=pltpu.CompilerParams(
            vmem_limit_bytes=63 * 2**20, collective_id=0, has_side_effects=True
        ),
        name="layer",
    )(att, residual, wo, wg, wu, wd)


def solution(mesh):
    n = mesh.shape["req"]

    def body(
        queries, new_key, new_value, key_cache, value_cache, lengths, page_table,
        residual, out_weight, gate_weight, up_weight, down_weight,
    ):
        att = attend(queries, new_key, new_value, key_cache, value_cache, lengths, page_table)
        return layer(n, att, residual, out_weight, gate_weight, up_weight, down_weight)

    return jax.shard_map(
        body,
        mesh=mesh,
        in_specs=(
            P("req", "head"),
            P("req", "head"),
            P("req", "head"),
            P("req", None, "head"),
            P("req", None, "head"),
            P("req"),
            P("req", None),
            P(None, ("head", "req")),
            P(None, ("head", "req")),
            P("head", "req"),
            P("head", "req"),
            P("req", "head"),
        ),
        out_specs=P(None, ("head", "req")),
        check_vma=False,
    )
```

time: 442 us -> 94.4 us (0.21)
  waiting for transfers between devices: 219 us -> 0 us
  local copies, waits for them, and re-layouts: 132 us -> 11.2 us
  Pallas kernels: 0 us -> 82.4 us
  matrix products: 69.2 us -> 0 us
  between operations: 13.2 us -> 0.04 us
    all_gather x2 -> x0, waiting for transfers between devices: 117 us -> none  [the longest x1 63.4 us: body(): lax.all_gather(features, 'req', axis=0, tiled=True)]
    reshape x2 -> x4, local copies, waits for them, and re-layouts: 92.1 us -> 2.96 us  [the longest x1 0.87 us: attend(): queries.astype(F32).reshape(rows, HD)]
    pallas_call x0 -> x2, Pallas kernels: none -> 82.4 us  [the longest x1 61.1 us: layer(): pl.pallas_call(functools.partial(layer_kernel, A, B), out_shape=jax.Shape...]
    reduce_scatter x1 -> x0, waiting for transfers between devices: 81.9 us -> none  [body(): lax.psum_scatter(lax.dot_general(down_weight, hidden, (((0,), (1,)), ((),...]
    dot_general x7 -> x0, matrix products: 69.2 us -> none  [the longest x1 20 us: attend_padded(): jnp.einsum('rgqt,rtgd->rgqd', weights, value_rows, preferred_element_type...]
    gather x2 -> x0, local copies, waits for them, and re-layouts: 37.9 us -> none  [the longest x1 19 us: attend_padded(): value_rows = value_pool[page_table].reshape(row_count, key_span, groups, HD)]
    psum x1 -> x0, waiting for transfers between devices: 19.8 us -> none  [body(): gate_full, up_full = lax.psum((gate_acts, up_acts), 'head')]
    unnamed x17 -> x9, local copies, waits for them, and re-layouts: 2.04 us -> 8.23 us
  transfers between devices with their start and end apart: 4 -> 0, of which waited for: 4 -> 0; matrix products, arithmetic and copies ran while one was open for 0% -> 0% of each run, Pallas kernels for 0% -> 0%
where the time goes in v1:
time: 94.4 us; the launch traced here: 93.6 us
  Pallas kernels  82.4 us (87%)
  local copies, waits for them, and re-layouts  11.2 us (12%)
    pallas_call x1, Pallas kernels, layer(): pl.pallas_call(functools.partial(layer_kernel, A, B), out_shape=jax.Shape...  61.1 us
    pallas_call x1, Pallas kernels, attend(): pl.pallas_call(functools.partial(attend_kernel, short), out_shape=jax.Sha...  21.3 us
    unnamed x9, local copies, waits for them, and re-layouts  8.23 us

profile of v1, /device:TPU:0, one launch (start us, length us, event | category | flops | bytes accessed | tf_op | source)
XLA Modules:
  0.0 93.6 jit_solution(13920914452745137140)
XLA Ops:
  0.0 0.7 reshape.32.nk_ref
  0.7 0.7 reshape.34.nv_ref
  1.4 0.9 reshape.30.q_ref
  2.3 0.0 copy-start
  2.3 2.7 %copy-done = bf16[92,64,512]{2,1,0:T(8,128)(2,1)S(1)} copy-done((bf16[92,64,512]{2,1,0:T(8,128)(2,1)S(1)}, bf16[92,64,512]{2,1,0:T(8,128)(2,1)}, u32[]{:S(2)}) %copy-start) | copy-done | bytes 6029336
  5.0 0.0 copy-start.1
  5.0 2.7 %copy-done.1 = bf16[92,64,512]{2,1,0:T(8,128)(2,1)S(1)} copy-done((bf16[92,64,512]{2,1,0:T(8,128)(2,1)S(1)}, bf16[92,64,512]{2,1,0:T(8,128)(2,1)}, u32[]{:S(2)}) %copy-start.1) | copy-done | bytes 6029336
  7.7 0.0 copy-start.2
  7.7 0.7 copy-done.2
  8.4 0.0 copy-start.3
  8.4 0.7 copy-done.3
  9.1 21.3 %attend.1 = bf16[256,128]{1,0:T(8,128)(2,1)S(1)} custom-call(s32[8]{0:T(128)S(1)} %copy-done.3, s32[8,64]{1,0:T(8,128)S(1)} %copy-done.2, f32[256,128]{1,0:T(8,128)S(1)} %reshape.30.q_ref, f32[32,128]{1,0:T(8,128)S(1)} %reshape.32.nk_ref, f32[32,128]{1,0:T(8,128)S(1)} %reshape.34.nv_ref, bf16[92,64,512]{2,1,0:T(8,128)(2,1)S(1)} %copy-done, ...), custom_call_target="tpu_custom_call" | custom-call | tf_op jit(solution)/shard_map/attend/pallas_call | solution.py:136
  30.4 0.7 copy.15
  31.0 61.1 %layer.1 = bf16[128,256]{1,0:T(8,128)(2,1)} custom-call(bf16[16,2048]{1,0:T(8,128)(2,1)} %bitcast.7, bf16[128,256]{1,0:T(8,128)(2,1)} %res_ref.1, bf16[8192,256]{1,0:T(8,128)(2,1)} %wo_hbm.1, bf16[4096,1792]{1,0:T(8,128)(2,1)} %wg_hbm.1, bf16[4096,1792]{1,0:T(8,128)(2,1)} %wu_hbm.1, bf16[1792,4096]{1,0:T(8,128)(2,1)} %wd_hbm.1), custom_call_target="tpu_custom_call" | custom-call | tf_op jit(solution)/shard_map/layer/pallas_call | solution.py:372
  92.2 1.5 %copy.17 = bf16[128,256]{1,0:T(8,128)(2,1)} copy(bf16[128,256]{1,0:T(8,128)(2,1)} %layer.1) | data formatting | bytes 131072
Async XLA Ops:
  2.3 2.7 %copy-start = (bf16[92,64,512]{2,1,0:T(8,128)(2,1)S(1)}, bf16[92,64,512]{2,1,0:T(8,128)(2,1)}, u32[]{:S(2)}) copy-start(bf16[92,64,512]{2,1,0:T(8,128)(2,1)} %keys.1) | copy-start | bytes 18087940
  5.0 2.7 %copy-start.1 = (bf16[92,64,512]{2,1,0:T(8,128)(2,1)S(1)}, bf16[92,64,512]{2,1,0:T(8,128)(2,1)}, u32[]{:S(2)}) copy-start(bf16[92,64,512]{2,1,0:T(8,128)(2,1)} %values.1) | copy-start | bytes 18087940
  7.7 0.7 copy-start.2
  8.4 0.7 copy-start.3

commit v2 on v1

--- a/solution.py
+++ b/solution.py
@@ -14,8 +14,8 @@
 
 
 def attend_kernel(
-    short_pages, lengths, table, q_ref, nk_ref, nv_ref, keys, values, out_ref,
-    ks, vs, kl, vl, s_ref, sl_ref, o_ref, sems,
+    short_pages, lengths, table, q_in, nk_in, nv_in, keys, values, out_ref,
+    q_ref, nk_ref, nv_ref, ks, vs, kl, vl, s_ref, sl_ref, o_ref, sems,
 ):
     reqs, slots = table.shape
     page = keys.shape[1]
@@ -48,6 +48,11 @@
             return carry
 
         lax.fori_loop(0, slots, start_long, 0)
+
+    heads = groups * per
+    for src, dst, count in ((q_in, q_ref, heads), (nk_in, nk_ref, groups), (nv_in, nv_ref, groups)):
+        for i in range(count):
+            dst[pl.ds(i, reqs, stride=count), :] = src[:, i * HD:(i + 1) * HD].astype(F32)
 
     def spread(ref):
         v = ref[...]
@@ -120,7 +125,10 @@
             ))
         o_ref[pl.ds(base, block), :] = jnp.concatenate(parts, axis=0) + added
 
-    out_ref[...] = o_ref[...].astype(BF16)
+    half = heads // 2
+    for i in range(half):
+        both = [o_ref[pl.ds(j * half + i, reqs, stride=heads), :] for j in range(2)]
+        out_ref[:, i * HD:(i + 1) * HD] = jnp.concatenate(both, axis=0).astype(BF16)
 
 
 def attend(queries, new_key, new_value, keys, values, lengths, table):
@@ -133,12 +141,15 @@
     smem = pl.BlockSpec(memory_space=pltpu.SMEM)
     vmem = pl.BlockSpec(memory_space=pltpu.VMEM)
     hbm = pl.BlockSpec(memory_space=pl.ANY)
-    out = pl.pallas_call(
+    return pl.pallas_call(
         functools.partial(attend_kernel, short),
-        out_shape=jax.ShapeDtypeStruct((rows, HD), BF16),
+        out_shape=jax.ShapeDtypeStruct((2 * reqs, queries.shape[1] // 2), BF16),
         in_specs=[smem, smem, vmem, vmem, vmem, hbm, hbm],
         out_specs=vmem,
         scratch_shapes=[
+            pltpu.VMEM((rows, HD), F32),
+            pltpu.VMEM((reqs * groups, HD), F32),
+            pltpu.VMEM((reqs * groups, HD), F32),
             pltpu.VMEM((reqs, short, page, width), BF16),
             pltpu.VMEM((reqs, short, page, width), BF16),
             pltpu.VMEM((slots, page, width), BF16),
@@ -148,17 +159,11 @@
             pltpu.VMEM((rows, HD), F32),
             pltpu.SemaphoreType.DMA((4,)),
         ],
-        compiler_params=pltpu.CompilerParams(vmem_limit_bytes=40 * 2**20),
+        compiler_params=pltpu.CompilerParams(vmem_limit_bytes=62 * 2**20),
         name="attend",
     )(
-        lengths, table,
-        queries.astype(F32).reshape(rows, HD),
-        new_key.astype(F32).reshape(reqs * groups, HD),
-        new_value.astype(F32).reshape(reqs * groups, HD),
-        keys, values,
+        lengths, table, queries, new_key, new_value, keys, values,
     )
-    half = per_req // 2
-    return out.reshape(reqs, 2, half, HD).transpose(1, 0, 2, 3).reshape(2 * reqs, half * HD)
 
 
 def layer_kernel(
@@ -206,36 +211,84 @@
     def source(da, db):
         return lax.rem(a + A - da, A) * B + lax.rem(b + B - db, B)
 
-    def gather_start(ref, sfar, rfar, snear, rnear, each):
-        fars = [None] + [
-            send(ref.at[idx], ref.at[idx], sfar.at[d], rfar.at[d], far(d)) for d in range(1, A)
-        ]
-        nears = {}
-        for da in range(A):
+    def plane(kind):
+        return a * B + (b + 1 - 2 * lax.rem(b, 2), b + 2 - 4 * (b // 2), B - 1 - b)[kind]
+
+    def source_plane(da, kind):
+        return lax.rem(a + A - da, A) * B + plane(kind) - a * B
+
+    sent = []
+
+    class Gather:
+        def __init__(self, ref, sems, cut):
+            self.ref, self.sems, self.cut = ref, sems, cut
+            self.near, self.part = {}, {}
+            self.far = [None] + [
+                self.go(ref.at[idx], (0, d), far(d)) for d in range(1, A)
+            ]
+
+        def go(self, src, at, to):
+            sfar, rfar, snear, rnear = self.sems
+            where = (sfar.at[at[1]], rfar.at[at[1]]) if at[0] == 0 else (
+                snear.at[at[1:]], rnear.at[at[1:]])
+            cp = send(src, src, *where, to)
+            sent.append(cp)
+            return cp
+
+        def spread(self, da):
             if da:
-                fars[da].wait_recv()
-            at = source(da, 0)
+                self.far[da].wait_recv()
+            src = self.ref.at[source(da, 0)]
+            if B == 4:
+                for kind in range(2):
+                    self.near[da, kind] = self.go(src, (1, da, kind), {"req": plane(kind)})
+            else:
+                for db in range(1, B):
+                    self.near[da, db] = self.go(src, (1, da, db), near(db))
+
+        def relay(self, da):
+            if B == 4:
+                for kind in range(2):
+                    self.near[da, kind].wait_recv()
+                    src = self.cut(source_plane(da, kind), kind)
+                    self.part[da, kind] = self.go(
+                        src, (1, da, 2 + kind), {"req": plane(1 - kind)}
+                    )
+                return [source_plane(da, kind) for kind in range(2)]
             for db in range(1, B):
-                nears[da, db] = send(
-                    ref.at[at], ref.at[at], snear.at[da, db], rnear.at[da, db], near(db)
-                )
-            each(da, at)
-        return fars, nears
+                self.near[da, db].wait_recv()
+            return [source(da, db) for db in range(1, B)]
+
+        def finish(self, da):
+            if B == 4:
+                for kind in range(2):
+                    self.part[da, kind].wait_recv()
+                return [source_plane(da, 2)]
+            return []
 
     forwards = {}
 
-    def forward(da, db, at):
-        forwards[da, db] = send(
-            att.at[0, at], att.at[1, at], ss.at[da, db], rs.at[da, db], sibling
-        )
-
-    fars, nears = gather_start(
-        att.at[0], sa, ra, sb, rb, lambda da, at: forward(da, 0, at)
+    def forward(da, where):
+        for at in where:
+            i = sum(k[0] == da for k in forwards)
+            forwards[da, i] = send(
+                att.at[0, at], att.at[1, at], ss.at[da, i], rs.at[da, i], sibling
+            )
+
+    first = Gather(
+        att.at[0], (sa, ra, sb, rb),
+        lambda at, i: att.at[0, at, :, i * (kh // 2):(i + 1) * (kh // 2)],
     )
     for da in range(A):
-        for db in range(1, B):
-            nears[da, db].wait_recv()
-            forward(da, db, source(da, db))
+        first.spread(da)
+        forward(da, [source(da, 0)])
+        if da:
+            forward(da - 1, first.relay(da - 1))
+        if da > 1:
+            forward(da - 2, first.finish(da - 2))
+    forward(A - 1, first.relay(A - 1))
+    for da in range(max(A - 2, 0), A):
+        forward(da, first.finish(da))
 
     loads[0].wait()
 
@@ -255,28 +308,18 @@
     update = update + project(1, 1 - h)
     mix[idx] = (res_ref[...].astype(F32) + update).astype(BF16)
 
-    mfars = [None] + [
-        send(mix.at[idx], mix.at[idx], sma.at[d], rma.at[d], far(d)) for d in range(1, A)
-    ]
-    mnears = {}
-
-    def spread(da):
-        if da:
-            mfars[da].wait_recv()
-        at = source(da, 0)
-        for db in range(1, B):
-            mnears[da, db] = send(
-                mix.at[at], mix.at[at], smb.at[da, db], rmb.at[da, db], near(db)
-            )
-
-    spread(0)
+    second = Gather(
+        mix, (sma, rma, smb, rmb),
+        lambda at, i: mix.at[at, i * (rows // 2):(i + 1) * (rows // 2), :],
+    )
+    second.spread(0)
+    if A > 1:
+        second.spread(1)
+    second.relay(0)
     loads[1].wait()
     loads[2].wait()
+    second.finish(0)
     for da in range(A):
-        for db in range(1, B):
-            mnears[da, db].wait_recv()
-        if da + 1 < A:
-            spread(da + 1)
         group = lax.rem(a + A - da, A) * B
 
         def do_tile(t, carry, da=da, group=group):
@@ -300,7 +343,15 @@
                 send(xs.at[t], xr.at[t], sx.at[t], rx.at[t], sibling)
             return carry
 
-        lax.fori_loop(0, tiles, do_tile, 0)
+        middle = (tiles + 1) // 2
+        lax.fori_loop(0, middle, do_tile, 0)
+        if da + 1 < A:
+            second.relay(da + 1)
+        if da + 2 < A:
+            second.spread(da + 2)
+        lax.fori_loop(middle, tiles, do_tile, 0)
+        if da + 1 < A:
+            second.finish(da + 1)
 
     for t in range(tiles):
         pltpu.make_async_remote_copy(
@@ -352,10 +403,7 @@
         total = total + r2[i].astype(F32)
     out_ref[...] = total.astype(BF16)
 
-    for cp in (
-        fars[1:] + list(nears.values()) + list(forwards.values()) + mfars[1:]
-        + list(mnears.values()) + list(firsts.values()) + seconds
-    ):
+    for cp in sent + list(forwards.values()) + list(firsts.values()) + seconds:
         cp.wait_send()
 
 

time: 94.4 us -> 75.1 us (0.80)
  local copies, waits for them, and re-layouts: 11.2 us -> 1.47 us
  Pallas kernels: 82.4 us -> 73.1 us
    pallas_call x1, Pallas kernels: 21.3 us -> 8.38 us  [attend(): pl.pallas_call(functools.partial(attend_kernel, short), out_shape=jax.Sha...]
    unnamed x9 -> x1, local copies, waits for them, and re-layouts: 8.23 us -> 1.47 us
    pallas_call x1, Pallas kernels: 61.1 us -> 64.8 us  [layer(): pl.pallas_call(functools.partial(layer_kernel, A, B), out_shape=jax.Shape...]
    reshape x4 -> x0, local copies, waits for them, and re-layouts: 2.96 us -> none  [the longest x1 0.87 us: attend(): queries.astype(F32).reshape(rows, HD)]
where the time goes in v2:
time: 75.1 us; the launch traced here: 74.6 us
  Pallas kernels  73.1 us (97%)
  local copies, waits for them, and re-layouts  1.47 us (2%)
    pallas_call x1, Pallas kernels, layer(): pl.pallas_call(functools.partial(layer_kernel, A, B), out_shape=jax.Shape...  64.8 us
    pallas_call x1, Pallas kernels, attend(): pl.pallas_call(functools.partial(attend_kernel, short), out_shape=jax.Sha...  8.38 us

profile of v2, /device:TPU:0, one launch (start us, length us, event | category | flops | bytes accessed | tf_op | source)
XLA Modules:
  0.0 74.6 jit_solution(10619146046401308176)
XLA Ops:
  0.0 8.4 %attend.1.att_ref = bf16[16,2048]{1,0:T(8,128)(2,1)} custom-call(s32[8]{0:T(128)} %lengths.1, s32[8,64]{1,0:T(8,128)} %table.1, bf16[8,4096]{1,0:T(8,128)(2,1)} %q_in.1, bf16[8,512]{1,0:T(8,128)(2,1)} %nk_in.1, bf16[8,512]{1,0:T(8,128)(2,1)} %nv_in.1, bf16[92,64,512]{2,1,0:T(8,128)(2,1)} %keys.1, bf16[92,64,512]{2,1,0:T(8,128)(2,1)} %values.1), custom_call_target="tpu_custom_call" | custom-call | tf_op jit(solution)/shard_map/attend/pallas_call | solution.py:144
  8.4 64.8 %layer.1 = bf16[128,256]{1,0:T(8,128)(2,1)} custom-call(bf16[16,2048]{1,0:T(8,128)(2,1)} %attend.1.att_ref, bf16[128,256]{1,0:T(8,128)(2,1)} %res_ref.1, bf16[8192,256]{1,0:T(8,128)(2,1)} %wo_hbm.1, bf16[4096,1792]{1,0:T(8,128)(2,1)} %wg_hbm.1, bf16[4096,1792]{1,0:T(8,128)(2,1)} %wu_hbm.1, bf16[1792,4096]{1,0:T(8,128)(2,1)} %wd_hbm.1), custom_call_target="tpu_custom_call" | custom-call | tf_op jit(solution)/shard_map/layer/pallas_call | solution.py:420
  73.2 1.5 %copy.14 = bf16[128,256]{1,0:T(8,128)(2,1)} copy(bf16[128,256]{1,0:T(8,128)(2,1)} %layer.1) | data formatting | bytes 131072
